TPU v7x, 128 devices: a whole 4x4x4 slice. The times are simulated.
128 devices in a mesh: slab: 8 (over z, core), space: 16 (over y, x).
Axes of the slice: x: 4, y: 4, z: 4, core: 2. Of those that a mesh axis runs over, the one named last changes fastest.
Arguments:
- frames: bfloat16 [128, 128, 128, 128], P('slab', 'space'), may hold values from -6 to 6
- frame_dest: int32 [128], replicated, may hold values from 0 to 127, as said below
- clip_lengths: int32 [8], replicated, may hold values from 1 to 32, 128 in all
- norm_gain: float32 [128], replicated, may hold values from 0.5 to 1.5
- conv_bias: float32 [128], replicated, may hold values from -3 to 3
- conv_weight: bfloat16 [3, 3, 3, 128, 128], replicated, may hold values from -0.109375 to 0.109375
Outputs:
- encoded: float32 [128, 128, 128, 128], P('slab', None, 'space')
Inputs may be any that keep to these rules, and one draw needn't show every extreme that they name: frame_dest is a permutation; for every two slab indices a and b exactly 2 of the frames a * 16 to a * 16 + 15 go to positions b * 16 to b * 16 + 15.
All inputs are finite; a program needn't handle non-finite values.
Results may differ from a plain program's by a relative error of at most 0.0014.
Values may be sent and summed in bfloat16 or wider, within the bound.
A program may use at most 128 MiB of HBM per device.

v0:
```python
import jax
import jax.numpy as jnp
from jax import lax
from jax.sharding import PartitionSpec as P


def passed_along(block, axis, distance):
    devices = range(lax.axis_size(axis))
    route = [(i - distance, i) for i in devices if i - distance in devices]
    return lax.ppermute(block, axis, route)


def with_halo(block, sides, width):
    for axis, dim in sides:
        count = lax.axis_size(axis)
        forward = [(i, i + 1) for i in range(count - 1)]
        backward = [(target, source) for source, target in forward]
        low = lax.ppermute(
            lax.slice_in_dim(block, block.shape[dim] - width, None, axis=dim), axis, forward
        )
        high = lax.ppermute(lax.slice_in_dim(block, 0, width, axis=dim), axis, backward)
        block = jnp.concatenate([low, block, high], axis=dim)
    return block


def clip_masks(clip_lengths, positions):
    starts = jnp.cumsum(clip_lengths) - clip_lengths
    first_frame = jnp.max(
        jnp.where(starts[None, :] <= positions[:, None], starts[None, :], 0), axis=1
    )
    lags = jnp.arange(3, dtype=jnp.int32)
    return (positions[:, None] - lags[None, :] >= first_frame[:, None]).astype(jnp.bfloat16)


def normalize(arranged, norm_gain):
    values = arranged.astype(jnp.float32)
    meansq = jnp.mean(values * values, axis=-1, keepdims=True)
    return jax.nn.silu(values * lax.rsqrt(meansq + 1e-06) * norm_gain).astype(jnp.bfloat16)


def spatial_conv(inputs, kernel, padding):
    return lax.conv_general_dilated(
        inputs,
        kernel,
        (1, 1),
        padding,
        dimension_numbers=("NHWC", "HWIO", "NHWC"),
        preferred_element_type=jnp.float32,
    )


def with_earlier(normed):
    count = normed.shape[0]
    earlier = passed_along(normed[count - 2 :], "slab", 1)
    return jnp.concatenate([earlier, normed], axis=0)


def causal_branch(padded, masks, conv_weight, conv_bias, padding):
    count = masks.shape[0]
    branch = None
    for frame_lag in range(3):
        taps_in = (
            padded[2 - frame_lag : 2 - frame_lag + count] * masks[:, frame_lag][:, None, None, None]
        )
        term = spatial_conv(taps_in, conv_weight[frame_lag], padding)
        branch = term if branch is None else branch + term
    return branch + conv_bias


def local(frames, frame_dest, clip_lengths, norm_gain, conv_bias, conv_weight):
    slab_count = lax.axis_size("slab")
    slab_frames = frames.shape[0]
    per_peer = slab_frames // slab_count
    slab_pos = lax.axis_index("slab")
    own_dest = lax.dynamic_slice_in_dim(frame_dest, slab_pos * slab_frames, slab_frames)
    ordering = jnp.argsort(own_dest)
    packed = jnp.take(frames, ordering, axis=0)
    positions = slab_pos * slab_frames + jnp.arange(slab_frames, dtype=jnp.int32)
    inverse = jnp.argsort(frame_dest)
    sources = jnp.take(inverse, positions)
    source_slab = sources // slab_frames
    dest_table = jnp.take(frame_dest.reshape(slab_count, slab_frames), source_slab, axis=0)
    arrival = jnp.sum(
        ((dest_table >= slab_pos * slab_frames) & (dest_table < positions[:, None])).astype(
            jnp.int32
        ),
        axis=1,
    )
    picks = source_slab * per_peer + arrival
    masks = clip_masks(clip_lengths, positions)
    received = lax.all_to_all(packed, "slab", split_axis=0, concat_axis=0, tiled=True)
    arranged = jnp.take(received, picks, axis=0)
    normed = normalize(arranged, norm_gain)
    extended = with_earlier(normed)
    padded = with_halo(extended, (("space", 1),), 1)
    branch = causal_branch(padded, masks, conv_weight, conv_bias, ((0, 0), (1, 1)))
    encoded = arranged.astype(jnp.float32) + branch
    return lax.all_to_all(encoded, "space", split_axis=2, concat_axis=1, tiled=True)


def solution(mesh):
    placed = (P("slab", "space", None, None), P(), P(), P(), P(), P())
    return jax.shard_map(
        local, mesh=mesh, in_specs=placed, out_specs=P("slab", None, "space", None), check_vma=False
    )
```

profile of v0, /device:TPU:66, one launch (start us, length us, event | category | flops | bytes accessed | tf_op | source)
XLA Modules:
  0.0 284.2 jit_solution(7487285228178824776)
XLA Ops:
  0.0 0.7 dynamic_slice.3
  0.7 1.2 sort.34
  2.0 5.3 %gather_fusion.2 = bf16[16,8,128,128]{3,2,1,0:T(8,128)(2,1)} fusion(bf16[16,8,128,128]{3,2,1,0:T(8,128)(2,1)} %param.8, s32[1024]{0:T(1024)S(1)} %pad_clamp_fusion.1), kind=kCustom, calls=%fused_computation.clone | custom fusion | bytes 8388672 | tf_op jit(solution)/shard_map/jit(_take)/gather | solution.py:77
  7.3 0.0 copy-start.4
  7.3 4.7 %broadcast_select_fusion = bf16[16,8,128,128]{3,2,1,0:T(8,128)(2,1)} fusion(bf16[16,8,128,128]{3,2,1,0:T(8,128)(2,1)} %gather_fusion.2, pred[16]{0:T(512)(128)(4,1)S(1)} %compare_and_fusion.1), kind=kLoop, calls=%fused_computation.23 | loop fusion | flops 2097152 | bytes 8388624 | tf_op jit(solution)/shard_map/jit(_take)/select_n | solution.py:77
  12.0 5.0 %all-to-all-start = ((bf16[16,8,128,128]{3,2,1,0:T(8,128)(2,1)}), bf16[16,8,128,128]{3,2,1,0:T(8,128)(2,1)}, u32[]{:S(2)}, u32[]{:S(2)}) async-start(bf16[16,8,128,128]{3,2,1,0:T(8,128)(2,1)} %broadcast_select_fusion), calls=%async_computation | async-start | bytes 8388608 | tf_op jit(solution)/shard_map/all_to_all | solution.py:91
  16.9 0.0 copy-done.4
  16.9 0.0 copy-start.3
  16.9 0.1 reshape.149
  17.0 2.5 sort.35
  19.6 0.7 gather_fusion
  20.3 0.6 gather_fusion.1
  20.9 0.2 convert_reduce_fusion
  21.1 42.5 %all-to-all-done = bf16[16,8,128,128]{3,2,1,0:T(8,128)(2,1)} async-done(((bf16[16,8,128,128]{3,2,1,0:T(8,128)(2,1)}), bf16[16,8,128,128]{3,2,1,0:T(8,128)(2,1)}, u32[]{:S(2)}, u32[]{:S(2)}) %all-to-all-start) | async-done | bytes 4194336 | tf_op jit(solution)/shard_map/all_to_all | solution.py:91
  63.6 5.2 %gather_fusion.3 = bf16[16,8,128,128]{3,2,1,0:T(8,128)(2,1)} fusion(bf16[16,8,128,128]{3,2,1,0:T(8,128)(2,1)} %all-to-all-done, s32[1024]{0:T(1024)S(1)} %pad_clamp_fusion), kind=kCustom, calls=%fused_computation.1.clone | custom fusion | bytes 8388672 | tf_op jit(solution)/shard_map/jit(_take)/gather | solution.py:92
  68.8 0.0 copy-start.6
  68.8 4.9 %fusion = f32[16,8,128]{0,2,1:T(8,128)S(1)} fusion(bf16[16,8,128,128]{3,2,1,0:T(8,128)(2,1)} %gather_fusion.3, pred[16]{0:T(512)(128)(4,1)S(1)} %get-tuple-element.10), kind=kLoop, calls=%fused_computation.7 | loop fusion | flops 8372224 | bytes 4259856 | tf_op jit(solution)/shard_map/reduce_sum | solution.py:37
  73.7 0.2 copy.33
  73.9 0.2 copy.34
  74.1 0.0 copy-done.3
  74.1 7.2 %fusion.7 = bf16[16,8,128,128]{3,0,2,1:T(8,128)(2,1)S(1)} fusion(f32[128]{0:T(128)S(1)} %copy-done.3, f32[16,8,128]{0,2,1:T(8,128)S(1)} %copy.34, bf16[16,8,128,128]{3,2,1,0:T(8,128)(2,1)} %gather_fusion.3, pred[16]{0:T(512)(128)(4,1)S(1)} %get-tuple-element.10), kind=kLoop, calls=%fused_computation.14 | loop fusion | flops 18874368 | bytes 8454672 | tf_op jit(solution)/shard_map/convert_element_type | solution.py:38
  81.3 0.0 copy-start
  81.3 2.0 copy-done
  83.3 0.5 slice.56
  83.9 1.9 collective-permute-start
  85.8 0.0 copy-done.6
  85.8 0.2 reduce-window.9
  86.0 0.0 copy-start.1
  86.0 8.4 %collective-permute-done = bf16[2,8,128,128]{3,0,2,1:T(2,128)(2,1)S(1)} collective-permute-done((bf16[2,8,128,128]{3,0,2,1:T(2,128)(2,1)S(1)}, bf16[2,8,128,128]{3,0,2,1:T(2,128)(2,1)S(1)}, u32[]{:S(2)}, u32[]{:S(2)}) %collective-permute-start) | collective-permute-done | bytes 524320 | tf_op jit(solution)/shard_map/ppermute | solution.py:10
  94.4 1.9 pad_maximum_fusion.2
  96.3 0.1 copy.35
  96.4 0.1 copy.36
  96.5 2.4 collective-permute-start.2
  98.9 3.6 %collective-permute-start.1 = (bf16[18,1,128,128]{3,2,1,0:T(8,128)(2,1)S(1)}, bf16[18,1,128,128]{3,2,1,0:T(8,128)(2,1)S(1)}, u32[]{:S(2)}, u32[]{:S(2)}) collective-permute-start(bf16[18,1,128,128]{3,2,1,0:T(8,128)(2,1)S(1)} %copy.35), channel_id=1, source_target_pairs={{0,1},{1,2},{2,3},{3,4},{4,5},{5,6},{6,7},{7,8},{8,9},{9,10},{10,1... | collective-permute-start | bytes 1769480 | tf_op jit(solution)/shard_map/ppermute | solution.py:18
  102.5 0.1 select_reduce_fusion
  102.6 10.9 %collective-permute-done.2 = bf16[18,1,128,128]{3,2,1,0:T(8,128)(2,1)S(1)} collective-permute-done((bf16[18,1,128,128]{3,2,1,0:T(8,128)(2,1)S(1)}, bf16[18,1,128,128]{3,2,1,0:T(8,128)(2,1)S(1)}, u32[]{:S(2)}, u32[]{:S(2)}) %collective-permute-start.2) | collective-permute-done | bytes 589856 | tf_op jit(solution)/shard_map/ppermute | solution.py:21
  113.5 0.4 copy.38
  113.9 0.0 copy-start.5
  113.9 1.7 collective-permute-done.1
  115.7 0.4 copy.37
  116.1 0.0 copy-done.1
  116.1 3.0 %pad_maximum_fusion = bf16[18,10,128,128]{3,0,2,1:T(8,128)(2,1)S(1)} fusion(bf16[18,1,128,128]{3,0,2,1:T(8,128)(2,1)S(1)} %copy.38, bf16[16,8,128,128]{3,0,2,1:T(8,128)(2,1)S(1)} %copy-done.1, bf16[2,8,128,128]{3,0,2,1:T(2,128)(2,1)S(1)} %collective-permute-done, bf16[18,1,128,128]{3,0,2,1:T(8,128)(2,1)S(1)} %copy.37), kind=kLoop, calls=%fused_computation.15 | loop fusion | flops 23592960 | bytes 11796480 | tf_op jit(solution)/shard_map/concatenate | solution.py:22
  119.2 0.0 copy-done.5
  119.2 12.3 %fusion.9 = f32[16,8,128,128]{3,0,2,1:T(8,128)} fusion(bf16[18,10,128,128]{3,0,2,1:T(8,128)(2,1)S(1)} %pad_maximum_fusion, bf16[16]{0:T(256)(128)(2,1)S(1)} %get-tuple-element.17, bf16[3,3,3,128,128]{4,3,2,1,0:T(8,128)(2,1)S(1)} %copy-done.5), kind=kOutput, calls=%fused_computation.19 | convolution fusion | flops 4817158144 | bytes 13926912 | tf_op jit(solution)/shard_map/conv_general_dilated | solution.py:42
  131.5 0.0 copy-start.2
  131.5 0.0 copy-start.7
  131.5 12.3 %fusion.10 = f32[16,8,128,128]{3,0,2,1:T(8,128)} fusion(bf16[18,10,128,128]{3,0,2,1:T(8,128)(2,1)S(1)} %pad_maximum_fusion, bf16[16]{0:T(256)(128)(2,1)S(1)} %get-tuple-element.18, bf16[3,3,3,128,128]{4,3,2,1,0:T(8,128)(2,1)S(1)} %copy-done.5), kind=kOutput, calls=%fused_computation.21 | convolution fusion | flops 4817158144 | bytes 13926912 | tf_op jit(solution)/shard_map/conv_general_dilated | solution.py:42
  143.8 0.0 copy-done.2
  143.8 0.0 copy-done.7
  143.8 23.1 %convert_add_fusion = f32[16,8,128,128]{3,0,2,1:T(8,128)} fusion(f32[16,8,128,128]{3,0,2,1:T(8,128)} %fusion.10, f32[16,8,128,128]{3,0,2,1:T(8,128)} %fusion.9, f32[128]{0:T(128)S(1)} %copy-done.7, bf16[18,10,128,128]{3,0,2,1:T(8,128)(2,1)S(1)} %pad_maximum_fusion, bf16[16]{0:T(256)(128)(2,1)S(1)} %get-tuple-element.16, ...), kind=kOutput, calls=%fused_computation.4 | convolution fusion | flops 4829741056 | bytes 34899456 | tf_op jit(solution)/shard_map/conv_general_dilated | solution.py:42
  166.8 4.4 %copy.39 = f32[16,8,128,128]{3,0,1,2:T(8,128)S(1)} copy(f32[16,8,128,128]{3,0,2,1:T(8,128)} %convert_add_fusion) | data formatting | bytes 16777216 | tf_op jit(solution)/shard_map/add | solution.py:97
  171.3 104.7 %all_to_all.23 = f32[16,8,128,128]{3,0,1,2:T(8,128)S(1)} all-to-all(f32[16,8,128,128]{3,0,1,2:T(8,128)S(1)} %copy.39), channel_id=1, replica_groups=mesh['slab'=8,'space'=16] {'space'}, dimensions={2} | all-to-all | bytes 16777216 | tf_op jit(solution)/shard_map/all_to_all | solution.py:98
  275.9 8.3 %copy.40 = f32[16,16,8,8,128]{4,3,2,1,0:T(8,128)} copy(f32[16,16,8,8,128]{4,0,2,3,1:T(8,128)S(1)} %bitcast.30) | data formatting | bytes 16777216 | tf_op jit(solution)/shard_map/all_to_all | solution.py:98
  (17 shorter events, 0.2 us)
Async XLA Ops:
  7.3 9.6 %copy-start.4 = (s32[128]{0:T(128)S(1)}, s32[128]{0:T(128)}, u32[]{:S(2)}) copy-start(s32[128]{0:T(128)} %param.9) | copy-start | bytes 1540
  12.0 51.6 %all-to-all-start = ((bf16[16,8,128,128]{3,2,1,0:T(8,128)(2,1)}), bf16[16,8,128,128]{3,2,1,0:T(8,128)(2,1)}, u32[]{:S(2)}, u32[]{:S(2)}) async-start(bf16[16,8,128,128]{3,2,1,0:T(8,128)(2,1)} %broadcast_select_fusion), calls=%async_computation | async-start | bytes 8388608 | tf_op jit(solution)/shard_map/all_to_all | solution.py:91
  16.9 57.2 %copy-start.3 = (f32[128]{0:T(128)S(1)}, f32[128]{0:T(128)}, u32[]{:S(2)}) copy-start(f32[128]{0:T(128)} %param.11) | copy-start | bytes 1540
  68.8 17.0 %copy-start.6 = (s32[8]{0:T(128)S(1)}, s32[8]{0:T(128)}, u32[]{:S(2)}) copy-start(s32[8]{0:T(128)} %param.10) | copy-start | bytes 100
  81.3 2.0 copy-start
  83.9 10.5 %collective-permute-start = (bf16[2,8,128,128]{3,0,2,1:T(2,128)(2,1)S(1)}, bf16[2,8,128,128]{3,0,2,1:T(2,128)(2,1)S(1)}, u32[]{:S(2)}, u32[]{:S(2)}) collective-permute-start(bf16[2,8,128,128]{3,0,2,1:T(2,128)(2,1)S(1)} %slice.56), channel_id=1, source_target_pairs={{0,16},{16,32},{32,48},{48,64},{64,80},{80,96},{96,112},{1,17},{17... | collective-permute-start | bytes 1572872 | tf_op jit(solution)/shard_map/ppermute | solution.py:10
  86.0 30.1 %copy-start.1 = (bf16[16,8,128,128]{3,0,2,1:T(8,128)(2,1)S(1)}, bf16[16,8,128,128]{3,0,2,1:T(8,128)(2,1)}, u32[]{:S(2)}) copy-start(bf16[16,8,128,128]{3,0,2,1:T(8,128)(2,1)} %copy-done) | copy-start | bytes 12582916
  96.5 17.0 %collective-permute-start.2 = (bf16[18,1,128,128]{3,2,1,0:T(8,128)(2,1)S(1)}, bf16[18,1,128,128]{3,2,1,0:T(8,128)(2,1)S(1)}, u32[]{:S(2)}, u32[]{:S(2)}) collective-permute-start(bf16[18,1,128,128]{3,2,1,0:T(8,128)(2,1)S(1)} %copy.36), channel_id=1, source_target_pairs={{1,0},{2,1},{3,2},{4,3},{5,4},{6,5},{7,6},{8,7},{9,8},{10,9},{11,1... | collective-permute-start | bytes 1769480 | tf_op jit(solution)/shard_map/ppermute | solution.py:21
  98.9 16.7 %collective-permute-start.1 = (bf16[18,1,128,128]{3,2,1,0:T(8,128)(2,1)S(1)}, bf16[18,1,128,128]{3,2,1,0:T(8,128)(2,1)S(1)}, u32[]{:S(2)}, u32[]{:S(2)}) collective-permute-start(bf16[18,1,128,128]{3,2,1,0:T(8,128)(2,1)S(1)} %copy.35), channel_id=1, source_target_pairs={{0,1},{1,2},{2,3},{3,4},{4,5},{5,6},{6,7},{7,8},{8,9},{9,10},{10,1... | collective-permute-start | bytes 1769480 | tf_op jit(solution)/shard_map/ppermute | solution.py:18
  113.9 5.2 %copy-start.5 = (bf16[3,3,3,128,128]{4,3,2,1,0:T(8,128)(2,1)S(1)}, bf16[3,3,3,128,128]{4,3,2,1,0:T(8,128)(2,1)}, u32[]{:S(2)}) copy-start(bf16[3,3,3,128,128]{4,3,2,1,0:T(8,128)(2,1)} %param.13) | copy-start | bytes 2654212
  131.5 12.3 %copy-start.2 = (bf16[16,8,128,128]{3,2,1,0:T(8,128)(2,1)S(1)}, bf16[16,8,128,128]{3,2,1,0:T(8,128)(2,1)}, u32[]{:S(2)}) copy-start(bf16[16,8,128,128]{3,2,1,0:T(8,128)(2,1)} %gather_fusion.3) | copy-start | bytes 12582916
  131.5 12.3 %copy-start.7 = (f32[128]{0:T(128)S(1)}, f32[128]{0:T(128)}, u32[]{:S(2)}) copy-start(f32[128]{0:T(128)} %param.12) | copy-start | bytes 1540
where the time goes:
time: 285 us; the launch traced here: 284 us
  blocking collectives  105 us (37%)
  waiting for transfers between devices  63.5 us (22%)
  matrix products  47.7 us (17%)
  local copies, waits for them, and re-layouts  29.2 us (10%)
  other arithmetic  26 us (9%)
  starting transfers between devices  12.9 us (5%)
    all_to_all x1, blocking collectives, local(): lax.all_to_all(encoded, 'space', split_axis=2, concat_axis=1, tiled=True)  105 us
    conv_general_dilated x3, matrix products, spatial_conv(): lax.conv_general_dilated(inputs, kernel, (1, 1), padding, dimension_numbe...  47.7 us
    all_to_all x1, waiting for transfers between devices, local(): lax.all_to_all(packed, 'slab', split_axis=0, concat_axis=0, tiled=True)  42.5 us
    ppermute x1, waiting for transfers between devices, with_halo(): lax.ppermute(lax.slice_in_dim(block, 0, width, axis=dim), axis, backward)  10.9 us
    ppermute x1, waiting for transfers between devices, passed_along(): return lax.ppermute(block, axis, route)  8.38 us
    all_to_all x1, local copies, waits for them, and re-layouts, local(): lax.all_to_all(encoded, 'space', split_axis=2, concat_axis=1, tiled=True)  8.25 us
    convert_element_type x1, other arithmetic, normalize(): jax.nn.silu(values * lax.rsqrt(meansq + 1e-06) * norm_gain)  7.2 us
  transfers between devices with their start and end apart: 4, of which 4 were waited for; matrix products, arithmetic and copies ran while one was open for 2% of the time, Pallas kernels for 0%

commit v1 on v0

v1 whole, which is shorter than its diff:
```python
import functools

import jax
import jax.numpy as jnp
from jax import lax
from jax.experimental import pallas as pl
from jax.experimental.pallas import tpu as pltpu
from jax.sharding import PartitionSpec as P

MESH = pl.DeviceIdType.MESH
BF, F32 = jnp.bfloat16, jnp.float32
CH = 128
BAND = 8
PARTS = BAND + 2
AHEAD = 2


def shape_of_space(count):
    side = int(count**0.5)
    return (side, side) if side * side == count else (1, count)


def kernel(
    NS, SY, SX, frames, index, mask, gain, bias, weight, out,
    fr, st, packed, recv, stag, arr, xs, tsend, trecv, wraw, wbig, outv,
    send_sem, recv_sem, tsend_sem, trecv_sem, out_sem, edge_sem, frame_sem, weight_sem,
):
    SP = SY * SX
    TF = 2 * NS
    width = fr.shape[2]
    pairs = 2 if SY > 1 else 1
    groups = SP // pairs
    a = lax.axis_index("slab")
    s = lax.axis_index("space")
    y, x = s // SX, lax.rem(s, SX)

    def loop(count, body, start=0):
        lax.fori_loop(start, count, lambda i, _: (body(i), 0)[1], 0)

    def offset(g, u):
        return g // SX + 2 * u, lax.rem(lax.rem(g, SX) + 2 * u, SX)

    def target(g, u):
        dy, dx = offset(g, u)
        return lax.rem(y + dy, SY) * SX + lax.rem(x + dx, SX)

    def source(g, u):
        dy, dx = offset(g, u)
        return lax.rem(y - dy + SY, SY) * SX + lax.rem(x - dx + SX, SX)

    def group_of(band):
        dy = lax.rem(y - band // SX + SY, SY)
        dx = lax.rem(x - lax.rem(band, SX) + SX, SX)
        u = dy // 2
        return (dy - 2 * u) * SX + lax.rem(dx - 2 * u + 2 * SX, SX)

    def block_copy(c, b, band, slab):
        return pltpu.make_async_remote_copy(
            src_ref=packed.at[c, b], dst_ref=recv.at[band, slab],
            send_sem=send_sem.at[c, b], recv_sem=recv_sem.at[band, slab],
            device_id=(b, c), device_id_type=MESH,
        )

    def tail_copy(band):
        return pltpu.make_async_remote_copy(
            src_ref=tsend.at[band], dst_ref=trecv.at[band],
            send_sem=tsend_sem.at[band], recv_sem=trecv_sem.at[band],
            device_id=(lax.rem(a + 1, NS), s), device_id_type=MESH,
        )

    def frame_copy(i):
        return pltpu.make_async_copy(frames.at[i], fr.at[i], frame_sem.at[i])

    loop(TF, lambda i: frame_copy(i).start())
    weight_copy = pltpu.make_async_copy(weight, wraw, weight_sem)
    weight_copy.start()
    barrier = pltpu.get_barrier_semaphore()

    def greet(i):
        pl.semaphore_signal(
            barrier, inc=1, device_id_type=MESH,
            device_id=(lax.rem(a + i // SP, NS), lax.rem(s + lax.rem(i, SP), SP)),
        )

    loop(NS * SP, greet, 1)
    loop(TF, lambda i: frame_copy(i).wait())

    def pack(b):
        for j in range(2):
            i = index[2 * b + j]
            for h in range(BAND):
                st[j, h * width : (h + 1) * width] = fr[i, h].astype(F32)

        def strip(c):
            for h in range(BAND):
                at = pl.ds(pl.multiple_of(h * width + c * BAND, BAND), BAND)
                packed[c, b, h] = jnp.concatenate([st[0, at], st[1, at]], axis=0).astype(BF)
            for side in range(2):
                if side:
                    column = jnp.minimum(c * BAND + BAND, width - 1)
                    inside = (c < SP - 1).astype(F32)
                else:
                    column = jnp.maximum(c * BAND - 1, 0)
                    inside = (c > 0).astype(F32)
                at = pl.ds(column, BAND, stride=width)
                both = jnp.concatenate([st[0, at], st[1, at]], axis=0)
                packed[c, b, BAND + side] = (both * inside).astype(BF)

        loop(SP, strip)

    loop(NS, pack)
    recv[s, a] = packed[s, a]
    pl.semaphore_wait(barrier, NS * SP - 1)

    def send_group(g):
        count = NS * pairs

        def one(j):
            m = lax.rem(5 * j + 3, count)
            b = lax.rem(a + m // pairs, NS)
            c = target(g, lax.rem(m, pairs))

            @pl.when(jnp.logical_or(b != a, c != s))
            def _():
                block_copy(c, b, s, a).start()

        loop(count, one)

    for g in range(min(AHEAD, groups)):
        send_group(g)

    weight_copy.wait()
    rows = 3 * CH
    for lag in range(3):
        for r in range(4):
            for o in range(2):
                at = (lag, slice(r * rows, (r + 1) * rows), slice(o * CH, (o + 1) * CH))
                if 0 <= r - o <= 2:
                    wbig[at] = wraw[lag, r - o]
                else:
                    wbig[at] = jnp.zeros((rows, CH), BF)
    for r in (0, 1, SP * BAND + 2, SP * BAND + 3):
        xs[r] = jnp.zeros(xs.shape[1:], BF)

    gains = gain[...]
    lines = lax.broadcasted_iota(jnp.int32, (BAND, CH), 0)

    def normalized(v):
        meansq = jnp.mean(v * v, axis=-1, keepdims=True)
        v = v * lax.rsqrt(meansq + 1e-06) * gains
        return 0.5 * v * (1.0 + jnp.tanh(0.5 * v))

    def shifted(body, before, after, h):
        first = jnp.broadcast_to(before[h : h + 1], (BAND, CH))
        last = jnp.broadcast_to(after[h : h + 1], (BAND, CH))
        return (
            jnp.where(lines == 0, first, pltpu.roll(body, 1, 0)),
            body,
            jnp.where(lines == BAND - 1, last, pltpu.roll(body, BAND - 1, 0)),
        )

    def arrive(band):
        def wait_one(k):
            @pl.when(jnp.logical_or(band != s, k != a))
            def _():
                block_copy(s, a, band, k).wait_recv()

        loop(NS, wait_one)

        def stage(k):
            for r in range(PARTS):
                v = recv[band, k, r].astype(F32)
                stag[2 * k, r] = v[:BAND]
                stag[2 * k + 1, r] = v[BAND:]

        loop(NS, stage)
        late, last = index[TF + TF - 2], index[TF + TF - 1]
        for r in range(PARTS):
            both = [normalized(stag[late, r]), normalized(stag[last, r])]
            tsend[band, r] = jnp.concatenate(both, axis=0).astype(BF)
        tail_copy(band).start()

    def spread(band):
        def frame(t):
            parts = []
            for f in range(2):
                slot = index[TF + t + f * NS]
                raw = [stag[slot, r] for r in range(PARTS)]
                parts.append((raw, [normalized(v) for v in raw]))
            for h in range(BAND):
                line = band * BAND + h
                arr[line, t] = jnp.concatenate([parts[0][0][h], parts[1][0][h]], axis=0).astype(BF)
                views = [shifted(n[h], n[BAND], n[BAND + 1], h) for _, n in parts]
                for k in range(3):
                    xs[line + 2, t + 2, :, k * CH : (k + 1) * CH] = jnp.concatenate(
                        [views[0][k], views[1][k]], axis=0
                    ).astype(BF)

        loop(NS, frame)

    def earlier(band):
        tail_copy(band).wait_recv()
        parts = [trecv[band, r].astype(F32) for r in range(PARTS)]
        for q in range(2):
            cut = slice(q * BAND, (q + 1) * BAND)
            for h in range(BAND):
                line = band * BAND + h + 2
                views = shifted(parts[h][cut], parts[BAND][cut], parts[BAND + 1][cut], h)
                for k in range(3):
                    lanes = slice(k * CH, (k + 1) * CH)
                    own = xs[line, NS + q, :, lanes].astype(F32)[:BAND]
                    xs[line, q, :, lanes] = jnp.concatenate([views[k], own], axis=0).astype(BF)

    def conv(starts):
        total = None
        for lag in range(3):
            taps = [
                jnp.concatenate(
                    [xs[r0 + r, 2 - lag : 2 - lag + NS].reshape(NS * 16, rows) for r in range(4)], axis=1
                )
                for r0 in starts
            ]
            taps = taps[0] if len(taps) == 1 else jnp.concatenate(taps, axis=0)
            term = jnp.dot(taps, wbig[lag], preferred_element_type=F32)
            if lag:
                keep = mask[lag - 1].reshape(NS * 16, CH)
                keep = jnp.concatenate([keep, keep], axis=1)
                term = term * (keep if len(starts) == 1 else jnp.concatenate([keep] * len(starts), axis=0))
            total = term if total is None else total + term
        return total

    def put(value, line):
        value = value + bias[...] + arr[line].astype(F32).reshape(NS * 16, CH)
        value = value.reshape(NS, 2, BAND, CH)
        for f in range(2):
            outv[f * NS : (f + 1) * NS, line] = value[:, f]

    def inner_copy(band):
        at = pl.ds(band * BAND + 1, BAND - 2)
        return pltpu.make_async_copy(outv.at[:, at], out.at[:, at], out_sem.at[band])

    def edge_copy(e, lines):
        at = pl.ds(jnp.maximum(e * BAND - 1, 0), lines)
        return pltpu.make_async_copy(outv.at[:, at], out.at[:, at], edge_sem.at[e])

    def inner(band):
        total = conv([band * BAND + 2 + 2 * p for p in range(3)])
        for p in range(3):
            for o in range(2):
                value = total[p * NS * 16 : (p + 1) * NS * 16, o * CH : (o + 1) * CH]
                put(value, band * BAND + 1 + 2 * p + o)
        inner_copy(band).start()

    def edge(e):
        total = conv([e * BAND])

        @pl.when(e > 0)
        def _():
            put(total[:, :CH], e * BAND - 1)

        @pl.when(e < SP)
        def _():
            put(total[:, CH:], e * BAND)

        @pl.when(jnp.logical_and(e > 0, e < SP))
        def _():
            edge_copy(e, 2).start()

        @pl.when(jnp.logical_or(e == 0, e == SP))
        def _():
            edge_copy(e, 1).start()

    def finish(g):
        def each(u):
            band = source(g, u)
            earlier(band)
            inner(band)

        loop(pairs, each)

        def maybe(e):
            low = group_of(jnp.maximum(e - 1, 0))
            high = group_of(jnp.minimum(e, SP - 1))

            @pl.when(jnp.maximum(low, high) == g)
            def _():
                edge(e)

        loop(SP + 1, maybe)

    def step(g):
        @pl.when(g < groups)
        def _():
            def each(u):
                band = source(g, u)
                arrive(band)
                spread(band)

            loop(pairs, each)

            @pl.when(g + AHEAD < groups)
            def _():
                send_group(g + AHEAD)

        @pl.when(g > 0)
        def _():
            finish(g - 1)

    loop(groups + 1, step)

    def drain(i):
        c, b = i // NS, lax.rem(i, NS)

        @pl.when(jnp.logical_or(b != a, c != s))
        def _():
            block_copy(c, b, s, a).wait_send()

    loop(NS * SP, drain)

    def close(band):
        tail_copy(band).wait_send()
        inner_copy(band).wait()

    loop(SP, close)
    edge_copy(0, 1).wait()
    loop(SP, lambda e: edge_copy(e, 2).wait(), 1)
    edge_copy(SP, 1).wait()


def orders(frame_dest, clip_lengths, slabs, per_slab, slab):
    where = frame_dest.reshape(slabs, per_slab)
    slot = jnp.arange(2 * slabs, dtype=jnp.int32)
    lane = jnp.arange(per_slab, dtype=jnp.int32)
    own = lax.dynamic_index_in_dim(where, slab, 0, keepdims=False) // per_slab
    meant = own[None, :] == (slot // 2)[:, None]
    low = jnp.min(jnp.where(meant, lane[None, :], per_slab), axis=1)
    high = jnp.max(jnp.where(meant, lane[None, :], -1), axis=1)
    send = jnp.where(slot % 2 == 0, low, high)
    here = where // per_slab == slab
    first = jnp.min(jnp.where(here, lane[None, :], per_slab), axis=1)
    second = lane[None, :] != first[:, None]
    slots = 2 * jnp.arange(slabs, dtype=jnp.int32)[:, None] + second.astype(jnp.int32)
    position = slab * per_slab + lane
    hit = where[None, :, :] == position[:, None, None]
    pick = jnp.sum(jnp.where(hit, slots[None], 0), axis=(1, 2))
    index = jnp.concatenate([send, pick]).astype(jnp.int32)
    clips = jnp.arange(clip_lengths.shape[0], dtype=jnp.int32)
    starts = jnp.sum(jnp.where(clips[:, None] < clips[None, :], clip_lengths[:, None], 0), axis=0)
    begin = jnp.max(jnp.where(starts[None, :] <= position[:, None], starts[None, :], 0), axis=1)
    lags = jnp.arange(1, 3, dtype=jnp.int32)
    keep = (position[None, :] - lags[:, None] >= begin[None, :]).astype(F32)
    keep = keep.reshape(2, 2, slabs).transpose(0, 2, 1)[:, :, :, None, None]
    keep = jnp.broadcast_to(keep, (2, slabs, 2, BAND, CH)).reshape(2, slabs, 2 * BAND, CH)
    return index, keep


def local(frames, frame_dest, clip_lengths, norm_gain, conv_bias, conv_weight):
    NS, SP = lax.axis_size("slab"), lax.axis_size("space")
    SY, SX = shape_of_space(SP)
    TF, _, width, _ = frames.shape
    lines = SP * BAND
    index, mask = orders(frame_dest, clip_lengths, NS, TF, lax.axis_index("slab"))
    vmem = pl.BlockSpec(memory_space=pltpu.VMEM)
    held = pl.BlockSpec(memory_space=pl.ANY)
    V, D = pltpu.VMEM, pltpu.SemaphoreType.DMA
    blocks = (SP, NS, PARTS, 2 * BAND, CH)
    return pl.pallas_call(
        functools.partial(kernel, NS, SY, SX),
        out_shape=jax.ShapeDtypeStruct((TF, lines, BAND, CH), F32),
        in_specs=[held, pl.BlockSpec(memory_space=pltpu.SMEM), vmem, vmem, vmem, held],
        out_specs=held,
        scratch_shapes=[
            V((TF, BAND, width, CH), BF),
            V((2, BAND * width, CH), F32),
            V(blocks, BF),
            V(blocks, BF),
            V((TF, PARTS, BAND, CH), F32),
            V((lines, NS, 2 * BAND, CH), BF),
            V((lines + 4, NS + 2, 2 * BAND, 3 * CH), BF),
            V((SP, PARTS, 2 * BAND, CH), BF),
            V((SP, PARTS, 2 * BAND, CH), BF),
            V((3, 3, 3 * CH, CH), BF),
            V((3, 12 * CH, 2 * CH), BF),
            V((TF, lines, BAND, CH), F32),
            D((SP, NS)),
            D((SP, NS)),
            D((SP,)),
            D((SP,)),
            D((SP,)),
            D((SP + 1,)),
            D((TF,)),
            D,
        ],
        compiler_params=pltpu.CompilerParams(
            collective_id=0, has_side_effects=True, vmem_limit_bytes=60 * 2**20
        ),
        cost_estimate=pl.CostEstimate(flops=2 * 10**10, bytes_accessed=2 * 10**7, transcendentals=10**7),
    )(
        frames, index, mask, norm_gain.reshape(1, CH), conv_bias.reshape(1, CH),
        conv_weight.reshape(3, 3, 3 * CH, CH),
    )


def solution(mesh):
    placed = (P("slab", "space", None, None), P(), P(), P(), P(), P())
    return jax.shard_map(
        local, mesh=mesh, in_specs=placed, out_specs=P("slab", None, "space", None), check_vma=False
    )
```

time: 285 us -> 141 us (0.49)
  the two profiles are of different devices: /device:TPU:66 before, /device:TPU:17 now
where the time goes in v1:
time: 141 us; the launch traced here: 140 us
  Pallas kernels  129 us (91%)
  local copies, waits for them, and re-layouts  9.41 us (7%)
  other arithmetic  2.34 us (2%)
    pallas_call x1, Pallas kernels, local(): pl.pallas_call(functools.partial(kernel, NS, SY, SX), out_shape=jax.Shape...  129 us
    unnamed x1, local copies, waits for them, and re-layouts  7.59 us

profile of v1, /device:TPU:17, one launch (start us, length us, event | category | flops | bytes accessed | tf_op | source)
XLA Modules:
  0.0 140.4 jit_solution(10671457439286117520)
XLA Ops:
  0.0 0.7 select_reduce_fusion.2
  0.7 0.1 select_reduce_fusion.1
  0.8 0.1 ge.14
  0.9 0.1 copy.8
  1.0 0.1 fusion.2
  1.1 0.7 reshape.101
  1.8 0.1 select_reduce_fusion.3
  2.0 0.2 fusion.1
  2.2 0.1 convert_add_fusion
  2.2 0.4 select_reduce_fusion
  2.7 0.6 pad_add_fusion.index
  3.3 0.1 broadcast_in_dim.100
  3.3 0.1 broadcast_in_dim.101
  3.4 0.8 broadcast_in_dim.102.mask
  4.2 128.6 %shard_map.64 = f32[16,128,8,128]{3,2,1,0:T(8,128)} custom-call(bf16[16,8,128,128]{3,2,1,0:T(8,128)(2,1)} %frames.1, s32[32]{0:T(128)} %pad_add_fusion.index, f32[2,8,16,128]{3,2,1,0:T(8,128)} %broadcast_in_dim.102.mask, f32[1,128]{1,0:T(1,128)} %bitcast.8, f32[1,128]{1,0:T(1,128)} %bitcast.9, bf16[3,3,384,128]{3,2,1,0:T(8,128)(2,1)} %bitcast.7), custom_call_target="tpu_custom_call" | custom-call | flops 20000000000 | bytes 20000000 | tf_op jit(solution)/shard_map/pallas_call | solution.py:367
  132.8 7.6 %copy.10 = f32[16,128,8,128]{3,2,1,0:T(8,128)} copy(f32[16,128,8,128]{3,2,1,0:T(8,128)} %shard_map.64) | data formatting | bytes 16777216
  (7 shorter events, 0.0 us)

commit v2 on v1

--- a/solution.py
+++ b/solution.py
@@ -13,6 +13,7 @@
 BAND = 8
 PARTS = BAND + 2
 AHEAD = 2
+BEHIND = 1
 
 
 def shape_of_space(count):
@@ -21,9 +22,9 @@
 
 
 def kernel(
-    NS, SY, SX, frames, index, mask, gain, bias, weight, out,
-    fr, st, packed, recv, stag, arr, xs, tsend, trecv, wraw, wbig, outv,
-    send_sem, recv_sem, tsend_sem, trecv_sem, out_sem, edge_sem, frame_sem, weight_sem,
+    NS, SY, SX, frames, index, mask, gain, bias, weight, outv,
+    fr, st, packed, recv, stag, arr, xs, tsend, trecv, wraw, wbig,
+    send_sem, recv_sem, tsend_sem, trecv_sem, frame_sem, weight_sem,
 ):
     SP = SY * SX
     TF = 2 * NS
@@ -159,7 +160,7 @@
             jnp.where(lines == BAND - 1, last, pltpu.roll(body, BAND - 1, 0)),
         )
 
-    def arrive(band):
+    def wait_blocks(band):
         def wait_one(k):
             @pl.when(jnp.logical_or(band != s, k != a))
             def _():
@@ -167,6 +168,7 @@
 
         loop(NS, wait_one)
 
+    def arrive(band):
         def stage(k):
             for r in range(PARTS):
                 v = recv[band, k, r].astype(F32)
@@ -235,21 +237,12 @@
         for f in range(2):
             outv[f * NS : (f + 1) * NS, line] = value[:, f]
 
-    def inner_copy(band):
-        at = pl.ds(band * BAND + 1, BAND - 2)
-        return pltpu.make_async_copy(outv.at[:, at], out.at[:, at], out_sem.at[band])
-
-    def edge_copy(e, lines):
-        at = pl.ds(jnp.maximum(e * BAND - 1, 0), lines)
-        return pltpu.make_async_copy(outv.at[:, at], out.at[:, at], edge_sem.at[e])
-
     def inner(band):
         total = conv([band * BAND + 2 + 2 * p for p in range(3)])
         for p in range(3):
             for o in range(2):
                 value = total[p * NS * 16 : (p + 1) * NS * 16, o * CH : (o + 1) * CH]
                 put(value, band * BAND + 1 + 2 * p + o)
-        inner_copy(band).start()
 
     def edge(e):
         total = conv([e * BAND])
@@ -261,14 +254,6 @@
         @pl.when(e < SP)
         def _():
             put(total[:, CH:], e * BAND)
-
-        @pl.when(jnp.logical_and(e > 0, e < SP))
-        def _():
-            edge_copy(e, 2).start()
-
-        @pl.when(jnp.logical_or(e == 0, e == SP))
-        def _():
-            edge_copy(e, 1).start()
 
     def finish(g):
         def each(u):
@@ -291,6 +276,15 @@
     def step(g):
         @pl.when(g < groups)
         def _():
+            def first(u):
+                wait_blocks(source(g, u))
+
+            loop(pairs, first)
+
+            @pl.when(g + AHEAD < groups)
+            def _():
+                send_group(g + AHEAD)
+
             def each(u):
                 band = source(g, u)
                 arrive(band)
@@ -298,15 +292,11 @@
 
             loop(pairs, each)
 
-            @pl.when(g + AHEAD < groups)
-            def _():
-                send_group(g + AHEAD)
-
-        @pl.when(g > 0)
-        def _():
-            finish(g - 1)
-
-    loop(groups + 1, step)
+        @pl.when(g >= BEHIND)
+        def _():
+            finish(g - BEHIND)
+
+    loop(groups + BEHIND, step)
 
     def drain(i):
         c, b = i // NS, lax.rem(i, NS)
@@ -319,12 +309,8 @@
 
     def close(band):
         tail_copy(band).wait_send()
-        inner_copy(band).wait()
 
     loop(SP, close)
-    edge_copy(0, 1).wait()
-    loop(SP, lambda e: edge_copy(e, 2).wait(), 1)
-    edge_copy(SP, 1).wait()
 
 
 def orders(frame_dest, clip_lengths, slabs, per_slab, slab):
@@ -366,9 +352,9 @@
     blocks = (SP, NS, PARTS, 2 * BAND, CH)
     return pl.pallas_call(
         functools.partial(kernel, NS, SY, SX),
-        out_shape=jax.ShapeDtypeStruct((TF, lines, BAND, CH), F32),
+        out_shape=pltpu.VMEM((TF, lines, BAND, CH), F32),
         in_specs=[held, pl.BlockSpec(memory_space=pltpu.SMEM), vmem, vmem, vmem, held],
-        out_specs=held,
+        out_specs=vmem,
         scratch_shapes=[
             V((TF, BAND, width, CH), BF),
             V((2, BAND * width, CH), F32),
@@ -381,18 +367,15 @@
             V((SP, PARTS, 2 * BAND, CH), BF),
             V((3, 3, 3 * CH, CH), BF),
             V((3, 12 * CH, 2 * CH), BF),
-            V((TF, lines, BAND, CH), F32),
             D((SP, NS)),
             D((SP, NS)),
             D((SP,)),
             D((SP,)),
-            D((SP,)),
-            D((SP + 1,)),
             D((TF,)),
             D,
         ],
         compiler_params=pltpu.CompilerParams(
-            collective_id=0, has_side_effects=True, vmem_limit_bytes=60 * 2**20
+            collective_id=0, has_side_effects=True, vmem_limit_bytes=46 * 2**20
         ),
         cost_estimate=pl.CostEstimate(flops=2 * 10**10, bytes_accessed=2 * 10**7, transcendentals=10**7),
     )(

time: 141 us -> 118 us (0.84)
  the two profiles are of different devices: /device:TPU:17 before, /device:TPU:66 now
where the time goes in v2:
time: 118 us; the launch traced here: 117 us
  Pallas kernels  110 us (93%)
  local copies, waits for them, and re-layouts  5.22 us (4%)
  other arithmetic  2.45 us (2%)
    pallas_call x1, Pallas kernels, local(): pl.pallas_call(functools.partial(kernel, NS, SY, SX), out_shape=pltpu.VME...  110 us
    unnamed x1, local copies, waits for them, and re-layouts  3.4 us

profile of v2, /device:TPU:66, one launch (start us, length us, event | category | flops | bytes accessed | tf_op | source)
XLA Modules:
  0.0 117.5 jit_solution(6256788861261480094)
XLA Ops:
  0.0 0.7 select_reduce_fusion.2
  0.7 0.1 select_reduce_fusion.1
  0.8 0.1 ge.14
  0.9 0.1 copy.8
  1.0 0.1 fusion.2
  1.1 0.7 reshape.101
  1.8 0.1 select_reduce_fusion.3
  2.0 0.2 fusion.1
  2.2 0.1 convert_add_fusion
  2.2 0.4 select_reduce_fusion
  2.7 0.7 pad_add_fusion.index
  3.4 0.1 broadcast_in_dim.100
  3.4 0.1 broadcast_in_dim.101
  3.5 0.8 broadcast_in_dim.102.mask
  4.3 109.8 %shard_map.64 = f32[16,128,8,128]{3,2,1,0:T(8,128)S(1)} custom-call(bf16[16,8,128,128]{3,2,1,0:T(8,128)(2,1)} %frames.1, s32[32]{0:T(128)} %pad_add_fusion.index, f32[2,8,16,128]{3,2,1,0:T(8,128)} %broadcast_in_dim.102.mask, f32[1,128]{1,0:T(1,128)} %bitcast.8, f32[1,128]{1,0:T(1,128)} %bitcast.9, bf16[3,3,384,128]{3,2,1,0:T(8,128)(2,1)} %bitcast.7), custom_call_target="tpu_custom_call" | custom-call | flops 20000000000 | bytes 20000000 | tf_op jit(solution)/shard_map/pallas_call | solution.py:353
  114.1 3.4 %copy.10 = f32[16,128,8,128]{3,2,1,0:T(8,128)} copy(f32[16,128,8,128]{3,2,1,0:T(8,128)S(1)} %shard_map.64) | data formatting | bytes 16777216
  (7 shorter events, 0.0 us)

commit v3 on v2

--- a/solution.py
+++ b/solution.py
@@ -198,7 +198,7 @@
                         [views[0][k], views[1][k]], axis=0
                     ).astype(BF)
 
-        loop(NS, frame)
+        lax.fori_loop(0, NS, lambda i, _: (frame(i), 0)[1], 0, unroll=2)
 
     def earlier(band):
         tail_copy(band).wait_recv()

time: 118 us -> 117 us (level)
  no operation moved by 1% of the time
where the time goes in v3:
time: 117 us
  Pallas kernels  109 us (93%)
  local copies, waits for them, and re-layouts  5.22 us (4%)
  other arithmetic  2.45 us (2%)
    pallas_call x1, Pallas kernels, local(): pl.pallas_call(functools.partial(kernel, NS, SY, SX), out_shape=pltpu.VME...  109 us
    unnamed x1, local copies, waits for them, and re-layouts  3.4 us

profile of v3, /device:TPU:66, one launch (start us, length us, event | category | flops | bytes accessed | tf_op | source)
XLA Modules:
  0.0 117.0 jit_solution(8627277397688530228)
XLA Ops:
  0.0 0.7 select_reduce_fusion.2
  0.7 0.1 select_reduce_fusion.1
  0.8 0.1 ge.14
  0.9 0.1 copy.8
  1.0 0.1 fusion.2
  1.1 0.7 reshape.101
  1.8 0.1 select_reduce_fusion.3
  2.0 0.2 fusion.1
  2.2 0.1 convert_add_fusion
  2.2 0.4 select_reduce_fusion
  2.7 0.7 pad_add_fusion.index
  3.4 0.1 broadcast_in_dim.100
  3.4 0.1 broadcast_in_dim.101
  3.5 0.8 broadcast_in_dim.102.mask
  4.3 109.3 %shard_map.64 = f32[16,128,8,128]{3,2,1,0:T(8,128)S(1)} custom-call(bf16[16,8,128,128]{3,2,1,0:T(8,128)(2,1)} %frames.1, s32[32]{0:T(128)} %pad_add_fusion.index, f32[2,8,16,128]{3,2,1,0:T(8,128)} %broadcast_in_dim.102.mask, f32[1,128]{1,0:T(1,128)} %bitcast.8, f32[1,128]{1,0:T(1,128)} %bitcast.9, bf16[3,3,384,128]{3,2,1,0:T(8,128)(2,1)} %bitcast.7), custom_call_target="tpu_custom_call" | custom-call | flops 20000000000 | bytes 20000000 | tf_op jit(solution)/shard_map/pallas_call | solution.py:353
  113.6 3.4 %copy.10 = f32[16,128,8,128]{3,2,1,0:T(8,128)} copy(f32[16,128,8,128]{3,2,1,0:T(8,128)S(1)} %shard_map.64) | data formatting | bytes 16777216
  (7 shorter events, 0.0 us)

commit v4 on v3

--- a/solution.py
+++ b/solution.py
@@ -175,7 +175,7 @@
                 stag[2 * k, r] = v[:BAND]
                 stag[2 * k + 1, r] = v[BAND:]
 
-        loop(NS, stage)
+        lax.fori_loop(0, NS, lambda i, _: (stage(i), 0)[1], 0, unroll=2)
         late, last = index[TF + TF - 2], index[TF + TF - 1]
         for r in range(PARTS):
             both = [normalized(stag[late, r]), normalized(stag[last, r])]

time: 117 us -> 117 us (level)
  no operation moved by 1% of the time
where the time goes in v4:
time: 117 us
  Pallas kernels  109 us (93%)
  local copies, waits for them, and re-layouts  5.22 us (4%)
  other arithmetic  2.45 us (2%)
    pallas_call x1, Pallas kernels, local(): pl.pallas_call(functools.partial(kernel, NS, SY, SX), out_shape=pltpu.VME...  109 us
    unnamed x1, local copies, waits for them, and re-layouts  3.4 us

profile of v4, /device:TPU:66, one launch (start us, length us, event | category | flops | bytes accessed | tf_op | source)
XLA Modules:
  0.0 117.1 jit_solution(183712651173772135)
XLA Ops:
  0.0 0.7 select_reduce_fusion.2
  0.7 0.1 select_reduce_fusion.1
  0.8 0.1 ge.14
  0.9 0.1 copy.8
  1.0 0.1 fusion.2
  1.1 0.7 reshape.101
  1.8 0.1 select_reduce_fusion.3
  2.0 0.2 fusion.1
  2.2 0.1 convert_add_fusion
  2.2 0.4 select_reduce_fusion
  2.7 0.7 pad_add_fusion.index
  3.4 0.1 broadcast_in_dim.100
  3.4 0.1 broadcast_in_dim.101
  3.5 0.8 broadcast_in_dim.102.mask
  4.3 109.4 %shard_map.64 = f32[16,128,8,128]{3,2,1,0:T(8,128)S(1)} custom-call(bf16[16,8,128,128]{3,2,1,0:T(8,128)(2,1)} %frames.1, s32[32]{0:T(128)} %pad_add_fusion.index, f32[2,8,16,128]{3,2,1,0:T(8,128)} %broadcast_in_dim.102.mask, f32[1,128]{1,0:T(1,128)} %bitcast.8, f32[1,128]{1,0:T(1,128)} %bitcast.9, bf16[3,3,384,128]{3,2,1,0:T(8,128)(2,1)} %bitcast.7), custom_call_target="tpu_custom_call" | custom-call | flops 20000000000 | bytes 20000000 | tf_op jit(solution)/shard_map/pallas_call | solution.py:353
  113.7 3.4 %copy.10 = f32[16,128,8,128]{3,2,1,0:T(8,128)} copy(f32[16,128,8,128]{3,2,1,0:T(8,128)S(1)} %shard_map.64) | data formatting | bytes 16777216
  (7 shorter events, 0.0 us)

commit v5 on v3

--- a/solution.py
+++ b/solution.py
@@ -112,6 +112,16 @@
     loop(NS, pack)
     recv[s, a] = packed[s, a]
     pl.semaphore_wait(barrier, NS * SP - 1)
+
+    def drain_group(g):
+        def one(j):
+            b, c = j // pairs, target(g, lax.rem(j, pairs))
+
+            @pl.when(jnp.logical_or(b != a, c != s))
+            def _():
+                block_copy(c, b, s, a).wait_send()
+
+        loop(NS * pairs, one)
 
     def send_group(g):
         count = NS * pairs
@@ -292,20 +302,18 @@
 
             loop(pairs, each)
 
+        @pl.when(jnp.logical_and(g >= 2, g < groups))
+        def _():
+            drain_group(g - 2)
+
         @pl.when(g >= BEHIND)
         def _():
             finish(g - BEHIND)
 
     loop(groups + BEHIND, step)
 
-    def drain(i):
-        c, b = i // NS, lax.rem(i, NS)
-
-        @pl.when(jnp.logical_or(b != a, c != s))
-        def _():
-            block_copy(c, b, s, a).wait_send()
-
-    loop(NS * SP, drain)
+    for g in range(max(groups - 2, 0), groups):
+        drain_group(g)
 
     def close(band):
         tail_copy(band).wait_send()

time: 117 us -> 116 us (level)
    pallas_call x1, Pallas kernels: 109 us -> 108 us  [local(): pl.pallas_call(functools.partial(kernel, NS, SY, SX), out_shape=pltpu.VME...]
where the time goes in v5:
time: 116 us
  Pallas kernels  108 us (93%)
  local copies, waits for them, and re-layouts  5.22 us (4%)
  other arithmetic  2.45 us (2%)
    pallas_call x1, Pallas kernels, local(): pl.pallas_call(functools.partial(kernel, NS, SY, SX), out_shape=pltpu.VME...  108 us
    unnamed x1, local copies, waits for them, and re-layouts  3.4 us

profile of v5, /device:TPU:66, one launch (start us, length us, event | category | flops | bytes accessed | tf_op | source)
XLA Modules:
  0.0 115.7 jit_solution(6047665202502787014)
XLA Ops:
  0.0 0.7 select_reduce_fusion.2
  0.7 0.1 select_reduce_fusion.1
  0.8 0.1 ge.14
  0.9 0.1 copy.8
  1.0 0.1 fusion.2
  1.1 0.7 reshape.101
  1.8 0.1 select_reduce_fusion.3
  2.0 0.2 fusion.1
  2.2 0.1 convert_add_fusion
  2.2 0.4 select_reduce_fusion
  2.7 0.7 pad_add_fusion.index
  3.4 0.1 broadcast_in_dim.100
  3.4 0.1 broadcast_in_dim.101
  3.5 0.8 broadcast_in_dim.102.mask
  4.3 108.0 %shard_map.64 = f32[16,128,8,128]{3,2,1,0:T(8,128)S(1)} custom-call(bf16[16,8,128,128]{3,2,1,0:T(8,128)(2,1)} %frames.1, s32[32]{0:T(128)} %pad_add_fusion.index, f32[2,8,16,128]{3,2,1,0:T(8,128)} %broadcast_in_dim.102.mask, f32[1,128]{1,0:T(1,128)} %bitcast.8, f32[1,128]{1,0:T(1,128)} %bitcast.9, bf16[3,3,384,128]{3,2,1,0:T(8,128)(2,1)} %bitcast.7), custom_call_target="tpu_custom_call" | custom-call | flops 20000000000 | bytes 20000000 | tf_op jit(solution)/shard_map/pallas_call | solution.py:361
  112.3 3.4 %copy.10 = f32[16,128,8,128]{3,2,1,0:T(8,128)} copy(f32[16,128,8,128]{3,2,1,0:T(8,128)S(1)} %shard_map.64) | data formatting | bytes 16777216
  (7 shorter events, 0.0 us)
